TPU v7x, 128 devices: a whole 4x4x4 slice. The times are simulated.
128 devices in a mesh: section: 4 (over x_lo, core), fsdp: 32 (over x_hi, z, y).
Axes of the slice: x: 4 (x_hi: 2, x_lo: 2; x = x_hi * 2 + x_lo), y: 4, z: 4, core: 2. Of those that a mesh axis runs over, the one named last changes fastest.
Arguments:
- saved_inputs: bfloat16 [4, 2, 32, 512, 1536], P('section', None, 'fsdp'), may hold values from -6 to 6
- grad_outputs: bfloat16 [2, 32, 512, 1536], P(None, 'fsdp'), may hold values from -6 to 6
- lengths: int32 [2, 32], P(None, 'fsdp'), may hold values from 256 to 512, as said below
- pointwise: bfloat16 [4, 1536, 1536], P('section', 'fsdp'), may hold values from -0.15625 to 0.15625
- depth_kernel: bfloat16 [4, 5, 1536], P('section', None, 'fsdp'), may hold values from -2.5 to 2.5
- norm_gain: bfloat16 [4, 1536], P('section', 'fsdp'), may hold values from 0.5 to 1.5
Outputs:
- frame_grads: bfloat16 [4, 2, 32, 512, 1536], P('section', None, 'fsdp')
- pointwise_grad: float32 [4, 1536, 1536], P('section', 'fsdp')
- kernel_grad: float32 [4, 5, 1536], P('section', None, 'fsdp')
- gain_grad: float32 [4, 1536], P('section', 'fsdp')
Inputs may be any that keep to these rules, and one draw needn't show every extreme that they name: `lengths`: frames at and after an utterance's length are padding; some utterance fills all 512 slots.
All inputs are finite; a program needn't handle non-finite values.
Results may differ from a plain program's by a relative error of at most 0.0057.
Values may be sent and summed in bfloat16 or wider, within the bound.
No kernel may reach another device: no remote copies, remote signals or barrier semaphores. Data moves between devices by JAX's collectives and lax.ppermute only.
A program may use at most 128 MiB of HBM per device.

v0:
```python
import jax
import jax.numpy as jnp
from jax import lax
from jax.sharding import PartitionSpec as P

EPSILON = 1e-05


def shifted(block, axis, distance):
    devices = range(lax.axis_size(axis))
    route = [(i - distance, i) for i in devices if i - distance in devices]
    return lax.ppermute(block, axis, route)


def depthwise(signal, kernel):
    tap_count = kernel.shape[0]
    margin = (tap_count - 1) // 2
    length = signal.shape[-2]
    widths = [(0, 0)] * (signal.ndim - 2) + [(margin, margin), (0, 0)]
    padded = jnp.pad(signal, widths)
    running = jnp.zeros(signal.shape, jnp.float32)
    for offset in range(tap_count):
        running = (
            running + kernel[offset].astype(jnp.float32) * padded[..., offset : offset + length, :]
        )
    return running


def tap_sums(upstream, signal, tap_count):
    margin = (tap_count - 1) // 2
    length = signal.shape[-2]
    widths = [(0, 0)] * (signal.ndim - 2) + [(margin, margin), (0, 0)]
    padded = jnp.pad(signal, widths)
    leading = tuple(range(signal.ndim - 1))
    return jnp.stack(
        [
            jnp.sum(upstream * padded[..., offset : offset + length, :], axis=leading)
            for offset in range(tap_count)
        ]
    )


def activation(inputs, present, kernel, gains):
    hidden = inputs.astype(jnp.float32) * present
    mixed = depthwise(hidden, kernel)
    average = jnp.mean(mixed, axis=-1, keepdims=True)
    centred = mixed - average
    inverse = lax.rsqrt(jnp.mean(centred * centred, axis=-1, keepdims=True) + EPSILON)
    normed = centred * inverse
    gained = normed * gains.astype(jnp.float32)
    logistic = jax.nn.sigmoid(gained)
    return (hidden, inverse, normed, gained, logistic)


def through_norm(
    grad_activated, hidden, inverse, normed, gained, logistic, kernel, gains, upstream, present
):
    grad_gained = grad_activated * (logistic + gained * logistic * (1.0 - logistic))
    leading = tuple(range(grad_gained.ndim - 1))
    gain_term = jnp.sum(grad_gained * normed, axis=leading)
    grad_normed = grad_gained * gains.astype(jnp.float32)
    grad_mixed = inverse * (
        grad_normed
        - jnp.mean(grad_normed, axis=-1, keepdims=True)
        - normed * jnp.mean(grad_normed * normed, axis=-1, keepdims=True)
    )
    kernel_term = tap_sums(grad_mixed, hidden, kernel.shape[0])
    grad_hidden = depthwise(grad_mixed, kernel[::-1])
    grad_inputs = (upstream + grad_hidden * present).astype(jnp.bfloat16)
    return (grad_inputs, kernel_term, gain_term)


def body(saved_inputs, grad_outputs, lengths, pointwise, depth_kernel, norm_gain):
    sections = lax.axis_size("section")
    section_id = lax.axis_index("section")
    local_inputs = saved_inputs[0, :, 0]
    local_grads = grad_outputs[:, 0]
    local_lengths = lengths[:, 0]
    micro_count, frames, features = local_inputs.shape
    factor = float(lax.axis_size("fsdp") * micro_count * frames) ** (-0.5)
    projection, kernel, gains = (
        lax.all_gather(pointwise[0], "fsdp", axis=0, tiled=True),
        lax.all_gather(depth_kernel[0], "fsdp", axis=1, tiled=True),
        lax.all_gather(norm_gain[0], "fsdp", axis=0, tiled=True),
    )
    places = jnp.arange(frames, dtype=jnp.int32)
    stores = (jnp.zeros((features, features), jnp.float32),)

    def compute_step(bundle):
        frame_out, kernel_sum, gain_sum, held, micro_slot, upstream_raw = bundle
        inputs = lax.dynamic_index_in_dim(local_inputs, micro_slot, 0, keepdims=False)
        length_now = lax.dynamic_index_in_dim(local_lengths, micro_slot, 0, keepdims=False)
        present = (places < length_now).astype(jnp.float32)[:, None]
        upstream = upstream_raw.astype(jnp.float32)
        hidden, inverse, normed, gained, logistic = activation(inputs, present, kernel, gains)
        activated = (gained * logistic).astype(jnp.bfloat16)
        grad_masked = (upstream * present).astype(jnp.bfloat16)
        grad_activated = lax.dot_general(
            grad_masked, projection, (((1,), (1,)), ((), ())), preferred_element_type=jnp.float32
        )
        grad_inputs, kernel_term, gain_term = through_norm(
            grad_activated,
            hidden,
            inverse,
            normed,
            gained,
            logistic,
            kernel,
            gains,
            upstream,
            present,
        )
        held = (
            held[0]
            + lax.dot_general(
                activated, grad_masked, (((0,), (0,)), ((), ())), preferred_element_type=jnp.float32
            ),
        )
        frame_out = lax.dynamic_update_index_in_dim(frame_out, grad_inputs, micro_slot, 0)
        return (grad_inputs, frame_out, kernel_sum + kernel_term, gain_sum + gain_term, held)

    def pass_step(bundle):
        frame_out, kernel_sum, gain_sum, held, micro_slot, upstream_raw = bundle
        return (jnp.zeros_like(upstream_raw), frame_out, kernel_sum, gain_sum, held)

    def one_turn(counter, loop_state):
        received, frame_out, kernel_sum, gain_sum, held = loop_state
        position = counter - (sections - 1 - section_id)
        active = jnp.logical_and(position >= 0, position < micro_count)
        micro_slot = jnp.clip(position, 0, micro_count - 1)
        outer_grad = lax.dynamic_index_in_dim(local_grads, micro_slot, 0, keepdims=False)
        upstream_raw = jnp.where(section_id == sections - 1, outer_grad, received)
        grad_inputs, frame_out, kernel_sum, gain_sum, held = lax.cond(
            active,
            compute_step,
            pass_step,
            (frame_out, kernel_sum, gain_sum, held, micro_slot, upstream_raw),
        )
        received = shifted(grad_inputs, "section", -1)
        return (received, frame_out, kernel_sum, gain_sum, held)

    initial = (
        jnp.zeros((frames, features), jnp.bfloat16),
        jnp.zeros((micro_count, frames, features), jnp.bfloat16),
        jnp.zeros(kernel.shape, jnp.float32),
        jnp.zeros((features,), jnp.float32),
        stores,
    )
    received, frame_out, kernel_sum, gain_sum, held = lax.fori_loop(
        0, micro_count + sections - 1, one_turn, initial
    )
    point_share, kernel_share, gain_share = (
        lax.psum_scatter(held[0], "fsdp", scatter_dimension=0, tiled=True),
        lax.psum_scatter(kernel_sum, "fsdp", scatter_dimension=1, tiled=True),
        lax.psum_scatter(gain_sum, "fsdp", scatter_dimension=0, tiled=True),
    )
    return (
        frame_out[None, :, None],
        (point_share * factor)[None],
        (kernel_share * factor)[None],
        (gain_share * factor)[None],
    )


def solution(mesh):
    placed = (
        P("section", None, "fsdp", None, None),
        P(None, "fsdp", None, None),
        P(None, "fsdp"),
        P("section", "fsdp", None),
        P("section", None, "fsdp"),
        P("section", "fsdp"),
    )
    return jax.shard_map(
        body,
        mesh=mesh,
        in_specs=placed,
        out_specs=(
            P("section", None, "fsdp", None, None),
            P("section", "fsdp", None),
            P("section", None, "fsdp"),
            P("section", "fsdp"),
        ),
        check_vma=False,
    )
```

profile of v0, /device:TPU:0, one launch (start us, length us, event | category | flops | bytes accessed | tf_op | source)
XLA Modules:
  0.0 916.9 jit_solution(1244989175964518420)
XLA Ops:
  8.8 102.0 %all-gather = bf16[1,5,1536]{1,0,2:T(2,128)(2,1)S(1)} all-gather(bf16[1,5,48]{1,0,2:T(2,128)(2,1)S(1)} %copy.13), channel_id=2, replica_groups=mesh['section'=4,'fsdp'=32] {'fsdp'}, dimensions={2}, use_global_device_ids=true | all-gather | bytes 15840 | tf_op jit(solution)/shard_map/all_gather | solution.py:83
  111.2 1.4 fusion.17
  114.1 88.9 %all-reduce.2 = bf16[1536]{0:T(1024)(128)(2,1)S(1)} all-reduce(bf16[1536]{0:T(1024)(128)(2,1)S(1)} %dynamic-update-slice), channel_id=4, replica_groups=mesh['section'=4,'fsdp'=32] {'fsdp'}, use_global_device_ids=true, to_apply=%add.2 | all-reduce | flops 1536 | bytes 6144 | tf_op jit(solution)/shard_map/all_gather | solution.py:84
  203.2 1.9 broadcast_in_dim.21
  205.1 4.8 broadcast_in_dim.42
  209.9 235.8 %while.24 = (s32[]{:T(128)}, bf16[512,1536]{1,0:T(8,128)(2,1)S(1)}, bf16[2,512,1536]{2,1,0:T(8,128)(2,1)}, f32[5,1536]{1,0:T(8,128)S(1)}, f32[1536]{0:T(1024)S(1...) while((s32[]{:T(128)}, bf16[512,1536]{1,0:T(8,128)(2,1)S(1)}, ...), condition=%wide.region_13.14_spmd.clone, body=%wide.region_0.13_spmd.clone.sunk | while | flops 4896336384 | bytes 110565944 | solution.py:149
  211.1 1.3 collective-permute-start
  212.4 4.2 collective-permute-done
  219.2 19.4 %collective-permute-done = bf16[512,1536]{1,0:T(8,128)(2,1)S(1)} collective-permute-done((bf16[512,1536]{1,0:T(8,128)(2,1)}, bf16[512,1536]{1,0:T(8,128)(2,1)S(1)}, u32[]{:S(2)}, u32[]{:S(2)}) %collective-permute-start) | collective-permute-done | bytes 1572896 | tf_op jit(solution)/shard_map/while/body/eval_jaxpr/ppermute | solution.py:12
  241.2 96.7 %collective-permute-done = bf16[512,1536]{1,0:T(8,128)(2,1)S(1)} collective-permute-done((bf16[512,1536]{1,0:T(8,128)(2,1)}, bf16[512,1536]{1,0:T(8,128)(2,1)S(1)}, u32[]{:S(2)}, u32[]{:S(2)}) %collective-permute-start) | collective-permute-done | bytes 1572896 | tf_op jit(solution)/shard_map/while/body/eval_jaxpr/ppermute | solution.py:12
  337.9 40.2 %conditional.3 = (bf16[512,1536]{1,0:T(8,128)(2,1)}, bf16[2,512,1536]{2,1,0:T(8,128)(2,1)}, f32[5,1536]{1,0:T(8,128)S(1)}, f32[1536]{0:T(1024)S(1)}, f32[1536,1536]{1,0:T(8,128)}) conditional(s32[]{:T(128)} %convert_element_type.106, (bf16[2,512,1536]{2,1,0:T(8,128)(2,1)}, f32[5,1536]{1,0:T(8,128)S(1)}, f32[1536]{0:T(1024)S(1)}, ...), branch_computations={%region_1.1_spmd, %region_2.12_spmd} | conditional | flops 4896336384 | bytes 104272064 | solution.py:133
  339.2 1.6 bitcast_select_fusion
  340.8 2.3 convert_multiply_fusion.1
  343.1 2.4 fusion.16
  346.0 3.6 multiply_reduce_fusion
  349.7 8.5 multiply_reduce_fusion.1
  358.3 9.3 %bitcast_dynamic-update-slice_fusion = (bf16[2,512,1536]{2,1,0:T(8,128)(2,1)}, bf16[512,1536]{1,0:T(8,128)(2,1)}) fusion(bf16[2,512,1536]{2,1,0:T(8,128)(2,1)} %get-tuple-element.440, s32[]{:T(128)S(6)} %min.10, f32[512]{0:T(512)S(1)} %compare_convert_fusion, f32[1536]{0:T(1024)S(1)} %get-tuple-element.546, f32[1536]{0:T(1024)S(1)} %get-tuple-element.545, ...), kind=kLoop, calls=%fused_computation.28 | loop fusion | flops 10223616 | bytes 7897092 | tf_op jit(solution)/shard_map/while/body/eval_jaxpr/cond/branch_1_fun/jit(dynamic_update_index_in_dim)/dynamic_update_slice | solution.py:119
  367.6 10.5 %convolution_add_fusion = f32[1536,1536]{1,0:T(8,128)} fusion(f32[1536,1536]{1,0:T(8,128)} %get-tuple-element.443, f32[512,1536]{1,0:T(8,128)S(1)} %get-tuple-element.579, f32[1536]{0:T(1024)S(1)} %convert_element_type.78, f32[512]{0:T(512)S(1)} %add_rsqrt_fusion, f32[512]{0:T(512)S(1)} %broadcast_multiply_fusion.2, bf16[512,1536]{1,0:T(8,128)(2,1)S(1)} %copy-done.1, ...), kind=kOutput, calls=%fused_computation.1 | convolution fusion | flops 2426929152 | bytes 23605248 | tf_op jit(solution)/shard_map/while/body/eval_jaxpr/cond/branch_1_fun/dot_general | solution.py:115
  379.4 20.6 %collective-permute-done = bf16[512,1536]{1,0:T(8,128)(2,1)S(1)} collective-permute-done((bf16[512,1536]{1,0:T(8,128)(2,1)}, bf16[512,1536]{1,0:T(8,128)(2,1)S(1)}, u32[]{:S(2)}, u32[]{:S(2)}) %collective-permute-start) | collective-permute-done | bytes 1572896 | tf_op jit(solution)/shard_map/while/body/eval_jaxpr/ppermute | solution.py:12
  400.0 40.2 %conditional.3 = (bf16[512,1536]{1,0:T(8,128)(2,1)}, bf16[2,512,1536]{2,1,0:T(8,128)(2,1)}, f32[5,1536]{1,0:T(8,128)S(1)}, f32[1536]{0:T(1024)S(1)}, f32[1536,1536]{1,0:T(8,128)}) conditional(s32[]{:T(128)} %convert_element_type.106, (bf16[2,512,1536]{2,1,0:T(8,128)(2,1)}, f32[5,1536]{1,0:T(8,128)S(1)}, f32[1536]{0:T(1024)S(1)}, ...), branch_computations={%region_1.1_spmd, %region_2.12_spmd} | conditional | flops 4896336384 | bytes 104272064 | solution.py:133
  401.4 1.6 bitcast_select_fusion
  403.0 2.3 convert_multiply_fusion.1
  405.3 2.4 fusion.16
  408.2 3.6 multiply_reduce_fusion
  411.8 8.5 multiply_reduce_fusion.1
  420.5 9.3 %bitcast_dynamic-update-slice_fusion = (bf16[2,512,1536]{2,1,0:T(8,128)(2,1)}, bf16[512,1536]{1,0:T(8,128)(2,1)}) fusion(bf16[2,512,1536]{2,1,0:T(8,128)(2,1)} %get-tuple-element.440, s32[]{:T(128)S(6)} %min.10, f32[512]{0:T(512)S(1)} %compare_convert_fusion, f32[1536]{0:T(1024)S(1)} %get-tuple-element.546, f32[1536]{0:T(1024)S(1)} %get-tuple-element.545, ...), kind=kLoop, calls=%fused_computation.28 | loop fusion | flops 10223616 | bytes 7897092 | tf_op jit(solution)/shard_map/while/body/eval_jaxpr/cond/branch_1_fun/jit(dynamic_update_index_in_dim)/dynamic_update_slice | solution.py:119
  429.7 10.5 %convolution_add_fusion = f32[1536,1536]{1,0:T(8,128)} fusion(f32[1536,1536]{1,0:T(8,128)} %get-tuple-element.443, f32[512,1536]{1,0:T(8,128)S(1)} %get-tuple-element.579, f32[1536]{0:T(1024)S(1)} %convert_element_type.78, f32[512]{0:T(512)S(1)} %add_rsqrt_fusion, f32[512]{0:T(512)S(1)} %broadcast_multiply_fusion.2, bf16[512,1536]{1,0:T(8,128)(2,1)S(1)} %copy-done.1, ...), kind=kOutput, calls=%fused_computation.1 | convolution fusion | flops 2426929152 | bytes 23605248 | tf_op jit(solution)/shard_map/while/body/eval_jaxpr/cond/branch_1_fun/dot_general | solution.py:115
  441.5 4.2 collective-permute-done
  448.3 92.5 %all-reduce.3 = f32[1536]{0:T(1024)S(1)} all-reduce(f32[1536]{0:T(1024)S(1)} %get-tuple-element.476), channel_id=7, replica_groups=mesh['section'=4,'fsdp'=32] {'fsdp'}, use_global_device_ids=true, to_apply=%region_16.17.clone | all-reduce | flops 1536 | bytes 12288
  541.5 122.3 %reduce-scatter.7.cloned.1.call-done = f32[48,5]{1,0:T(8,128)} async-done(((f32[1536,5]{1,0:T(8,128)}), f32[48,5]{1,0:T(8,128)}) %reduce-scatter.7.cloned.1.call-update) | async-done | bytes 976
  665.2 243.5 %reduce-scatter.5.cloned.1.call-done = f32[48,1536]{1,0:T(8,128)} async-done(((f32[1536,1536]{1,0:T(8,128)}), f32[48,1536]{1,0:T(8,128)}) %reduce-scatter.5.cloned.1.call-update) | async-done | bytes 294928 | tf_op jit(solution)/shard_map/reduce_scatter | solution.py:153
  908.7 1.7 multiply_bitcast_fusion
  (86 shorter events, 23.4 us)
Async XLA Ops:
  7.2 195.9 %all-gather.5.cloned.1.call-start = ((), (), s32[]{:S(2)}) async-start(), calls=%async_computation.3 | async-start | bytes 4866048 | tf_op jit(solution)/shard_map/all_gather | solution.py:82
  7.9 655.9 %reduce-scatter.7.cloned.1.call-start = ((), (), s32[]{:S(2)}) async-start(), calls=%async_computation.4 | async-start | bytes 811008
  205.1 4.8 copy-start.2
  211.1 5.5 collective-permute-start
  217.9 20.7 %collective-permute-start = (bf16[512,1536]{1,0:T(8,128)(2,1)}, bf16[512,1536]{1,0:T(8,128)(2,1)S(1)}, u32[]{:S(2)}, u32[]{:S(2)}) collective-permute-start(bf16[512,1536]{1,0:T(8,128)(2,1)} %get-tuple-element.675), channel_id=1, source_target_pairs={{32,0},{64,32},{96,64},{33,1},{65,33},{97,65},{34,2},{66,34},{98,6... | collective-permute-start | bytes 4718600 | tf_op jit(solution)/shard_map/while/body/eval_jaxpr/ppermute | solution.py:12
  239.9 98.0 %collective-permute-start = (bf16[512,1536]{1,0:T(8,128)(2,1)}, bf16[512,1536]{1,0:T(8,128)(2,1)S(1)}, u32[]{:S(2)}, u32[]{:S(2)}) collective-permute-start(bf16[512,1536]{1,0:T(8,128)(2,1)} %get-tuple-element.675), channel_id=1, source_target_pairs={{32,0},{64,32},{96,64},{33,1},{65,33},{97,65},{34,2},{66,34},{98,6... | collective-permute-start | bytes 4718600 | tf_op jit(solution)/shard_map/while/body/eval_jaxpr/ppermute | solution.py:12
  340.8 5.2 copy-start
  340.8 5.2 slice-start
  343.1 2.9 slice-start.1
  358.3 9.3 %copy-start.1 = (bf16[512,1536]{1,0:T(8,128)(2,1)S(1)}, bf16[512,1536]{1,0:T(8,128)(2,1)}, u32[]{:S(2)}) copy-start(bf16[512,1536]{1,0:T(8,128)(2,1)} %copy-done) | copy-start | bytes 4718596 | tf_op jit(solution)/shard_map/while/body/eval_jaxpr/cond
  378.1 21.9 %collective-permute-start = (bf16[512,1536]{1,0:T(8,128)(2,1)}, bf16[512,1536]{1,0:T(8,128)(2,1)S(1)}, u32[]{:S(2)}, u32[]{:S(2)}) collective-permute-start(bf16[512,1536]{1,0:T(8,128)(2,1)} %get-tuple-element.675), channel_id=1, source_target_pairs={{32,0},{64,32},{96,64},{33,1},{65,33},{97,65},{34,2},{66,34},{98,6... | collective-permute-start | bytes 4718600 | tf_op jit(solution)/shard_map/while/body/eval_jaxpr/ppermute | solution.py:12
  403.0 5.2 copy-start
  403.0 5.2 slice-start
  405.3 2.9 slice-start.1
  420.4 9.3 %copy-start.1 = (bf16[512,1536]{1,0:T(8,128)(2,1)S(1)}, bf16[512,1536]{1,0:T(8,128)(2,1)}, u32[]{:S(2)}) copy-start(bf16[512,1536]{1,0:T(8,128)(2,1)} %copy-done) | copy-start | bytes 4718596 | tf_op jit(solution)/shard_map/while/body/eval_jaxpr/cond
  440.2 5.5 collective-permute-start
  446.9 461.8 %reduce-scatter.5.cloned.1.call-start = ((), (), s32[]{:S(2)}) async-start(), calls=%async_computation.2 | async-start | bytes 9732096 | tf_op jit(solution)/shard_map/reduce_scatter | solution.py:153
Sparse Core Ops, SparseCore 0:
  11.0 86.2 all-gather.4
  447.0 216.7 reduce-scatter.6
  669.9 238.7 reduce-scatter.4
where the time goes:
time: 918 us; the launch traced here: 917 us
  waiting for transfers between devices  512 us (56%)
  blocking collectives  283 us (31%)
  other arithmetic  52.8 us (6%)
  matrix products  28.2 us (3%)
  local copies, waits for them, and re-layouts  18.1 us (2%)
  between operations  15.2 us (2%)
    reduce_scatter x1, waiting for transfers between devices, body(): lax.psum_scatter(held[0], 'fsdp', scatter_dimension=0, tiled=True)  243 us
    ppermute x5, waiting for transfers between devices, shifted(): return lax.ppermute(block, axis, route)  145 us
    unnamed x4, waiting for transfers between devices  124 us
    all_gather x1, blocking collectives, body(): lax.all_gather(depth_kernel[0], 'fsdp', axis=1, tiled=True)  102 us
    unnamed x1, blocking collectives  92.5 us
    all_gather x1, blocking collectives, body(): lax.all_gather(norm_gain[0], 'fsdp', axis=0, tiled=True)  88.9 us
    dot_general x2, matrix products, compute_step(): lax.dot_general(activated, grad_masked, (((0,), (0,)), ((), ())), preferr...  20.9 us
    dynamic_update_slice x2, other arithmetic, compute_step(): lax.dynamic_update_index_in_dim(frame_out, grad_inputs, micro_slot, 0)  18.5 us
  transfers between devices with their start and end apart: 8, of which 7 were waited for; matrix products, arithmetic and copies ran while one was open for 1% of the time, Pallas kernels for 0%

commit v1 on v0

--- a/solution.py
+++ b/solution.py
@@ -81,7 +81,9 @@
     projection, kernel, gains = (
         lax.all_gather(pointwise[0], "fsdp", axis=0, tiled=True),
         lax.all_gather(depth_kernel[0], "fsdp", axis=1, tiled=True),
-        lax.all_gather(norm_gain[0], "fsdp", axis=0, tiled=True),
+        jnp.concatenate(
+            lax.all_to_all(jnp.stack([norm_gain[0]] * lax.axis_size("fsdp")), "fsdp", 0, 0), axis=0
+        ),
     )
     places = jnp.arange(frames, dtype=jnp.int32)
     stores = (jnp.zeros((features, features), jnp.float32),)

time: 918 us -> 816 us (0.89)
  blocking collectives: 283 us -> 192 us
  other arithmetic: 52.8 us -> 33.2 us
  waiting for transfers between devices: 512 us -> 500 us
  local copies, waits for them, and re-layouts: 18.1 us -> 29.3 us
  starting transfers between devices: 6.52 us -> 17.4 us
    all_gather x1 -> x0, blocking collectives: 88.9 us -> none  [body(): lax.all_gather(norm_gain[0], 'fsdp', axis=0, tiled=True)]
    ppermute x5, waiting for transfers between devices: 145 us -> 133 us  [shifted(): return lax.ppermute(block, axis, route)]
    dynamic_update_slice x2, other arithmetic: 18.5 us -> 7.08 us  [compute_step(): lax.dynamic_update_index_in_dim(frame_out, grad_inputs, micro_slot, 0)]
    all_to_all x0 -> x1, starting transfers between devices: none -> 10.9 us  [body(): lax.all_to_all(jnp.stack([norm_gain[0]] * lax.axis_size('fsdp')), 'fsdp',...]
  transfers between devices with their start and end apart: 8 -> 9, of which waited for: 7 -> 7; matrix products, arithmetic and copies ran while one was open for 1% -> 1% of each run, Pallas kernels for 0% -> 0%
where the time goes in v1:
time: 816 us; the launch traced here: 815 us
  waiting for transfers between devices  500 us (61%)
  blocking collectives  192 us (24%)
  other arithmetic  33.2 us (4%)
  local copies, waits for them, and re-layouts  29.3 us (4%)
  matrix products  29 us (4%)
  starting transfers between devices  17.4 us (2%)
  between operations  14.5 us (2%)
    reduce_scatter x1, waiting for transfers between devices, body(): lax.psum_scatter(held[0], 'fsdp', scatter_dimension=0, tiled=True)  243 us
    ppermute x5, waiting for transfers between devices, shifted(): return lax.ppermute(block, axis, route)  133 us
    unnamed x4, waiting for transfers between devices  124 us
    all_gather x1, blocking collectives, body(): lax.all_gather(depth_kernel[0], 'fsdp', axis=1, tiled=True)  101 us
    unnamed x1, blocking collectives  90.7 us
    dot_general x2, matrix products, compute_step(): lax.dot_general(activated, grad_masked, (((0,), (0,)), ((), ())), preferr...  21.8 us
  transfers between devices with their start and end apart: 9, of which 7 were waited for; matrix products, arithmetic and copies ran while one was open for 1% of the time, Pallas kernels for 0%

profile of v1, /device:TPU:0, one launch (start us, length us, event | category | flops | bytes accessed | tf_op | source)
XLA Modules:
  0.0 815.0 jit_solution(10566512692849337958)
XLA Ops:
  9.2 10.9 %all-to-all-start = ((bf16[32,1,48]{2,1,0:T(2,128)(2,1)}), bf16[32,1,48]{2,1,0:T(2,128)(2,1)S(1)}, u32[]{:S(2)}, u32[]{:S(2)}) async-start(bf16[32,1,48]{2,1,0:T(2,128)(2,1)} %stack.33), calls=%async_computation | async-start | bytes 32768 | tf_op jit(solution)/shard_map/all_to_all | solution.py:85
  20.9 100.9 %all-gather = bf16[1,5,1536]{1,0,2:T(2,128)(2,1)S(1)} all-gather(bf16[1,5,48]{1,0,2:T(2,128)(2,1)S(1)} %copy.13), channel_id=2, replica_groups=mesh['section'=4,'fsdp'=32] {'fsdp'}, dimensions={2}, use_global_device_ids=true | all-gather | bytes 15840 | tf_op jit(solution)/shard_map/all_gather | solution.py:83
  123.7 1.9 broadcast_in_dim.21
  125.5 4.8 broadcast_in_dim.42
  130.4 214.8 %while.24 = (s32[]{:T(128)}, bf16[512,1536]{1,0:T(8,128)(2,1)}, bf16[2,512,1536]{2,1,0:T(8,128)(2,1)}, f32[5,1536]{1,0:T(8,128)S(1)}, f32[1536]{0:T(1024)S(1)}, ...) while((s32[]{:T(128)}, bf16[512,1536]{1,0:T(8,128)(2,1)}, ...), condition=%wide.region_13.14_spmd.clone, body=%wide.region_0.13_spmd.clone.sunk | while | flops 4896336384 | bytes 134158936 | solution.py:151
  130.4 1.3 conditional.3
  133.0 4.2 collective-permute-done
  138.3 1.3 conditional.3
  140.9 19.0 %collective-permute-done = bf16[512,1536]{1,0:T(8,128)(2,1)S(1)} collective-permute-done((bf16[512,1536]{1,0:T(8,128)(2,1)}, bf16[512,1536]{1,0:T(8,128)(2,1)S(1)}, u32[]{:S(2)}, u32[]{:S(2)}) %collective-permute-start) | collective-permute-done | bytes 1572896 | tf_op jit(solution)/shard_map/while/body/eval_jaxpr/ppermute | solution.py:12
  163.6 84.6 %collective-permute-done = bf16[512,1536]{1,0:T(8,128)(2,1)S(1)} collective-permute-done((bf16[512,1536]{1,0:T(8,128)(2,1)}, bf16[512,1536]{1,0:T(8,128)(2,1)S(1)}, u32[]{:S(2)}, u32[]{:S(2)}) %collective-permute-start) | collective-permute-done | bytes 1572896 | tf_op jit(solution)/shard_map/while/body/eval_jaxpr/ppermute | solution.py:12
  249.4 33.1 %conditional.3 = (bf16[512,1536]{1,0:T(8,128)(2,1)}, bf16[2,512,1536]{2,1,0:T(8,128)(2,1)}, f32[5,1536]{1,0:T(8,128)S(1)}, f32[1536]{0:T(1024)S(1)}, f32[1536,1536]{1,0:T(8,128)}) conditional(s32[]{:T(128)} %convert_element_type.106, (bf16[2,512,1536]{2,1,0:T(8,128)(2,1)}, f32[5,1536]{1,0:T(8,128)S(1)}, f32[1536]{0:T(1024)S(1)}, ...), branch_computations={%region_1.1_spmd, %region_2.12_spmd} | conditional | flops 4896336384 | bytes 121573568 | solution.py:135
  250.7 1.7 convert_multiply_fusion.1
  252.4 2.4 fusion.16
  256.4 1.4 copy-done.4
  257.7 3.6 multiply_reduce_fusion
  261.4 6.4 multiply_reduce_fusion.1
  267.8 3.5 bitcast_dynamic-update-slice_fusion
  271.5 10.9 %convolution_add_fusion = f32[1536,1536]{1,0:T(8,128)} fusion(f32[1536,1536]{1,0:T(8,128)} %get-tuple-element.443, f32[512,1536]{1,0:T(8,128)S(1)} %get-tuple-element.579, f32[1536]{0:T(1024)S(1)} %convert_element_type.78, f32[512]{0:T(512)S(1)} %add_rsqrt_fusion, f32[512]{0:T(512)S(1)} %broadcast_multiply_fusion.2, bf16[512,1536]{1,0:T(8,128)(2,1)} %copy-done, ...), kind=kOutput, calls=%fused_computation.1 | convolution fusion | flops 2426929152 | bytes 23605248 | tf_op jit(solution)/shard_map/while/body/eval_jaxpr/cond/branch_1_fun/dot_general | solution.py:117
  283.7 20.7 %collective-permute-done = bf16[512,1536]{1,0:T(8,128)(2,1)S(1)} collective-permute-done((bf16[512,1536]{1,0:T(8,128)(2,1)}, bf16[512,1536]{1,0:T(8,128)(2,1)S(1)}, u32[]{:S(2)}, u32[]{:S(2)}) %collective-permute-start) | collective-permute-done | bytes 1572896 | tf_op jit(solution)/shard_map/while/body/eval_jaxpr/ppermute | solution.py:12
  305.5 33.0 %conditional.3 = (bf16[512,1536]{1,0:T(8,128)(2,1)}, bf16[2,512,1536]{2,1,0:T(8,128)(2,1)}, f32[5,1536]{1,0:T(8,128)S(1)}, f32[1536]{0:T(1024)S(1)}, f32[1536,1536]{1,0:T(8,128)}) conditional(s32[]{:T(128)} %convert_element_type.106, (bf16[2,512,1536]{2,1,0:T(8,128)(2,1)}, f32[5,1536]{1,0:T(8,128)S(1)}, f32[1536]{0:T(1024)S(1)}, ...), branch_computations={%region_1.1_spmd, %region_2.12_spmd} | conditional | flops 4896336384 | bytes 121573568 | solution.py:135
  306.9 1.7 convert_multiply_fusion.1
  308.6 2.4 fusion.16
  312.5 1.4 copy-done.4
  313.9 3.6 multiply_reduce_fusion
  317.5 6.4 multiply_reduce_fusion.1
  324.0 3.5 bitcast_dynamic-update-slice_fusion
  327.7 10.9 %convolution_add_fusion = f32[1536,1536]{1,0:T(8,128)} fusion(f32[1536,1536]{1,0:T(8,128)} %get-tuple-element.443, f32[512,1536]{1,0:T(8,128)S(1)} %get-tuple-element.579, f32[1536]{0:T(1024)S(1)} %convert_element_type.78, f32[512]{0:T(512)S(1)} %add_rsqrt_fusion, f32[512]{0:T(512)S(1)} %broadcast_multiply_fusion.2, bf16[512,1536]{1,0:T(8,128)(2,1)} %copy-done, ...), kind=kOutput, calls=%fused_computation.1 | convolution fusion | flops 2426929152 | bytes 23605248 | tf_op jit(solution)/shard_map/while/body/eval_jaxpr/cond/branch_1_fun/dot_general | solution.py:117
  339.8 4.2 collective-permute-done
  348.4 90.7 %all-reduce.2 = f32[1536]{0:T(1024)S(1)} all-reduce(f32[1536]{0:T(1024)S(1)} %get-tuple-element.476), channel_id=6, replica_groups=mesh['section'=4,'fsdp'=32] {'fsdp'}, use_global_device_ids=true, to_apply=%region_16.17.clone | all-reduce | flops 1536 | bytes 12288
  439.7 122.1 %reduce-scatter.7.cloned.1.call-done = f32[48,5]{1,0:T(8,128)} async-done(((f32[1536,5]{1,0:T(8,128)}), f32[48,5]{1,0:T(8,128)}) %reduce-scatter.7.cloned.1.call-update) | async-done | bytes 976
  563.3 243.5 %reduce-scatter.5.cloned.1.call-done = f32[48,1536]{1,0:T(8,128)} async-done(((f32[1536,1536]{1,0:T(8,128)}), f32[48,1536]{1,0:T(8,128)}) %reduce-scatter.5.cloned.1.call-update) | async-done | bytes 294928 | tf_op jit(solution)/shard_map/reduce_scatter | solution.py:155
  806.8 1.7 multiply_bitcast_fusion
  (98 shorter events, 32.5 us)
Async XLA Ops:
  7.2 115.2 %all-gather.4.cloned.1.call-start = ((), (), s32[]{:S(2)}) async-start(), calls=%async_computation.4 | async-start | bytes 4866048 | tf_op jit(solution)/shard_map/all_gather | solution.py:82
  9.2 113.1 %all-to-all-start = ((bf16[32,1,48]{2,1,0:T(2,128)(2,1)}), bf16[32,1,48]{2,1,0:T(2,128)(2,1)S(1)}, u32[]{:S(2)}, u32[]{:S(2)}) async-start(bf16[32,1,48]{2,1,0:T(2,128)(2,1)} %stack.33), calls=%async_computation | async-start | bytes 32768 | tf_op jit(solution)/shard_map/all_to_all | solution.py:85
  20.1 541.8 %reduce-scatter.7.cloned.1.call-start = ((), (), s32[]{:S(2)}) async-start(), calls=%async_computation.5 | async-start | bytes 811008
  125.5 4.8 copy-start.5
  131.7 5.5 collective-permute-start
  137.2 1.1 copy-start.2
  139.6 20.3 %collective-permute-start = (bf16[512,1536]{1,0:T(8,128)(2,1)}, bf16[512,1536]{1,0:T(8,128)(2,1)S(1)}, u32[]{:S(2)}, u32[]{:S(2)}) collective-permute-start(bf16[512,1536]{1,0:T(8,128)(2,1)} %get-tuple-element.673), channel_id=1, source_target_pairs={{32,0},{64,32},{96,64},{33,1},{65,33},{97,65},{34,2},{66,34},{98,6... | collective-permute-start | bytes 4718600 | tf_op jit(solution)/shard_map/while/body/eval_jaxpr/ppermute | solution.py:12
  159.9 1.1 copy-start.2
  162.3 85.9 %collective-permute-start = (bf16[512,1536]{1,0:T(8,128)(2,1)}, bf16[512,1536]{1,0:T(8,128)(2,1)S(1)}, u32[]{:S(2)}, u32[]{:S(2)}) collective-permute-start(bf16[512,1536]{1,0:T(8,128)(2,1)} %get-tuple-element.673), channel_id=1, source_target_pairs={{32,0},{64,32},{96,64},{33,1},{65,33},{97,65},{34,2},{66,34},{98,6... | collective-permute-start | bytes 4718600 | tf_op jit(solution)/shard_map/while/body/eval_jaxpr/ppermute | solution.py:12
  248.2 1.1 copy-start.2
  252.4 2.9 copy-start.3
  254.8 1.4 copy-start.1
  255.3 2.5 copy-start.4
  257.7 10.1 %copy-start = (bf16[512,1536]{1,0:T(8,128)(2,1)}, bf16[512,1536]{1,0:T(8,128)(2,1)S(1)}, u32[]{:S(2)}) copy-start(bf16[512,1536]{1,0:T(8,128)(2,1)S(1)} %bitcast_select_fusion) | copy-start | bytes 4718596 | tf_op jit(solution)/shard_map/while/body/eval_jaxpr/cond
  282.4 21.9 %collective-permute-start = (bf16[512,1536]{1,0:T(8,128)(2,1)}, bf16[512,1536]{1,0:T(8,128)(2,1)S(1)}, u32[]{:S(2)}, u32[]{:S(2)}) collective-permute-start(bf16[512,1536]{1,0:T(8,128)(2,1)} %get-tuple-element.673), channel_id=1, source_target_pairs={{32,0},{64,32},{96,64},{33,1},{65,33},{97,65},{34,2},{66,34},{98,6... | collective-permute-start | bytes 4718600 | tf_op jit(solution)/shard_map/while/body/eval_jaxpr/ppermute | solution.py:12
  304.4 1.1 copy-start.2
  308.6 2.9 copy-start.3
  310.9 1.4 copy-start.1
  311.4 2.5 copy-start.4
  313.9 10.1 %copy-start = (bf16[512,1536]{1,0:T(8,128)(2,1)}, bf16[512,1536]{1,0:T(8,128)(2,1)S(1)}, u32[]{:S(2)}) copy-start(bf16[512,1536]{1,0:T(8,128)(2,1)S(1)} %bitcast_select_fusion) | copy-start | bytes 4718596 | tf_op jit(solution)/shard_map/while/body/eval_jaxpr/cond
  338.6 5.5 collective-permute-start
  344.1 1.1 copy-start.2
  346.4 460.3 %reduce-scatter.5.cloned.1.call-start = ((), (), s32[]{:S(2)}) async-start(), calls=%async_computation.3 | async-start | bytes 9732096 | tf_op jit(solution)/shard_map/reduce_scatter | solution.py:155
  346.5 0.7 copy-start.6
Sparse Core Ops, SparseCore 0:
  11.0 86.0 all-gather.3
  346.5 215.2 reduce-scatter.6
  568.0 238.7 reduce-scatter.4
